TPU v7x, 256 devices: a whole 4x4x8 slice. The times are simulated.
256 devices in a mesh: resp: 16 (over y, z_hi), ctx: 16 (over x, z_lo, core).
Axes of the slice: x: 4, y: 4, z: 8 (z_hi: 4, z_lo: 2; z = z_hi * 2 + z_lo), core: 2. Of those that a mesh axis runs over, the one named last changes fastest.
Arguments:
- queries: bfloat16 [16, 2048, 2560], P('resp', 'ctx'), may hold values from -96 to 96
- resp_keys: bfloat16 [16, 2048, 512], P('resp', 'ctx'), may hold values from -6 to 6
- resp_values: bfloat16 [16, 2048, 512], P('resp', 'ctx'), may hold values from -6 to 6
- prompt_keys: bfloat16 [512, 512], P('ctx'), may hold values from -6 to 6
- prompt_values: bfloat16 [512, 512], P('ctx'), may hold values from -6 to 6
- out_grad: bfloat16 [16, 2048, 2560], P('resp', 'ctx'), may hold values from -24 to 24
- lengths: int32 [16], P('resp'), may hold values from 256 to 2048, as said below
Outputs:
- attn_out: bfloat16 [16, 2048, 2560], P('resp', 'ctx')
- query_grad: bfloat16 [16, 2048, 2560], P('resp', 'ctx')
- resp_key_grad: bfloat16 [16, 2048, 512], P('resp', 'ctx')
- resp_value_grad: bfloat16 [16, 2048, 512], P('resp', 'ctx')
- prompt_key_grad: bfloat16 [512, 512], P('ctx')
- prompt_value_grad: bfloat16 [512, 512], P('ctx')
Inputs may be any that keep to these rules, and one draw needn't show every extreme that they name: `lengths`: some response has all 2048 tokens.
All inputs are finite; a program needn't handle non-finite values.
Results may differ from a plain program's by a relative error of at most 0.023.
Values may be sent and summed in bfloat16 or wider, within the bound.
A program may use at most 128 MiB of HBM per device.

v0:
```python
import math
import jax
import jax.numpy as jnp
from jax import lax
from jax.sharding import PartitionSpec as P

DH = 128
HQ = 20
HK = 4
NEG = -1e30


def score_block(query4, keys_blk, key_pos, row_pos, scale):
    keys3 = keys_blk.reshape(keys_blk.shape[0], query4.shape[1], query4.shape[3])
    raw = jnp.einsum("nkgd,mkd->kgnm", query4, keys3, preferred_element_type=jnp.float32) * scale
    allowed = key_pos[None, :] <= row_pos[:, None]
    return jnp.where(allowed[None, None], raw, jnp.float32(NEG))


def scan_blocks(keys_all, values_all, pos_all, step, init):
    total_rows = keys_all.shape[0]
    block = math.gcd(total_rows, 512)
    count = total_rows // block
    blocks = (
        keys_all.reshape(count, block, keys_all.shape[1]),
        values_all.reshape(count, block, values_all.shape[1]),
        pos_all.reshape(count, block),
    )
    return lax.scan(step, init, blocks)


def body(queries, resp_keys, resp_values, prompt_keys, prompt_values, out_grad, lengths):
    rows = queries.shape[1]
    group = HQ // HK
    width = HK * DH
    scale = DH ** (-0.5)
    cycle = lax.axis_size("ctx")
    first_row = lax.axis_index("ctx") * rows
    row_pos = first_row + jnp.arange(rows, dtype=jnp.int32)
    row_ok = row_pos < lengths[0]
    query4 = queries[0].reshape(rows, HK, group, DH)
    grad = jnp.where(row_ok[:, None], out_grad[0], jnp.zeros_like(out_grad[0]))
    grad4 = grad.reshape(rows, HK, group, DH)
    seq_rows = resp_keys.shape[1] * cycle
    prompt_rows = prompt_keys.shape[0] * cycle

    def stats_update(stats, keys_blk, key_pos):
        top, total = stats
        scores = score_block(query4, keys_blk, key_pos, row_pos, scale)
        new_top = jnp.maximum(top, jnp.max(scores, axis=-1))
        total = total * jnp.exp(top - new_top) + jnp.sum(
            jnp.exp(scores - new_top[..., None]), axis=-1
        )
        return (new_top, total)

    top0 = jnp.full((HK, group, rows), NEG, jnp.float32)
    total0 = jnp.zeros((HK, group, rows), jnp.float32)
    pieces = (
        lax.all_gather(prompt_keys, "ctx", axis=0, tiled=True),
        lax.all_gather(prompt_values, "ctx", axis=0, tiled=True),
    )
    top = top0
    total = total0
    key_pos = jnp.full((pieces[0].shape[0],), -1, jnp.int32)
    top, total = stats_update((top, total), pieces[0], key_pos)
    key_buf = pieces[0]
    value_buf = pieces[1]
    top, total, prompt_kbuf, prompt_vbuf = (top, total, key_buf, value_buf)
    pieces = (
        lax.all_gather(resp_keys[0], "ctx", axis=0, tiled=True),
        lax.all_gather(resp_values[0], "ctx", axis=0, tiled=True),
    )
    top, total, key_buf, value_buf = (
        top,
        total,
        jnp.zeros((seq_rows, width), jnp.bfloat16),
        jnp.zeros((seq_rows, width), jnp.bfloat16),
    )
    key_pos = jnp.arange(pieces[0].shape[0], dtype=jnp.int32)
    top, total = stats_update((top, total), pieces[0], key_pos)
    key_buf = pieces[0]
    value_buf = pieces[1]
    top, total, resp_kbuf, resp_vbuf = (top, total, key_buf, value_buf)
    lse = top + jnp.log(total)
    prompt_pos = jnp.full((prompt_rows,), -1, jnp.int32)
    resp_pos = jnp.arange(seq_rows, dtype=jnp.int32)

    def out_step(acc, blk):
        keys_blk, values_blk, key_pos = blk
        scores = score_block(query4, keys_blk, key_pos, row_pos, scale)
        prob = jnp.exp(scores - lse[..., None]).astype(jnp.bfloat16)
        values3 = values_blk.reshape(values_blk.shape[0], HK, DH)
        return (
            acc + jnp.einsum("kgnm,mkd->nkgd", prob, values3, preferred_element_type=jnp.float32),
            None,
        )

    mixed0 = jnp.zeros((rows, HK, group, DH), jnp.float32)
    mixed, unused = scan_blocks(prompt_kbuf, prompt_vbuf, prompt_pos, out_step, mixed0)
    mixed, unused = scan_blocks(resp_kbuf, resp_vbuf, resp_pos, out_step, mixed)
    attn_out = jnp.where(row_ok[:, None], mixed.reshape(rows, HQ * DH), jnp.float32(0.0)).astype(
        jnp.bfloat16
    )
    delta = jnp.einsum(
        "nkgd,nkgd->kgn",
        grad4,
        attn_out.reshape(rows, HK, group, DH),
        preferred_element_type=jnp.float32,
    )

    def grads_block(keys_blk, values_blk, key_pos):
        scores = score_block(query4, keys_blk, key_pos, row_pos, scale)
        prob = jnp.exp(scores - lse[..., None])
        prob_low = prob.astype(jnp.bfloat16)
        keys3 = keys_blk.reshape(keys_blk.shape[0], HK, DH)
        values3 = values_blk.reshape(values_blk.shape[0], HK, DH)
        dprob = jnp.einsum("nkgd,mkd->kgnm", grad4, values3, preferred_element_type=jnp.float32)
        dscore = (prob * (dprob - delta[..., None])).astype(jnp.bfloat16)
        dquery = (
            jnp.einsum("kgnm,mkd->nkgd", dscore, keys3, preferred_element_type=jnp.float32) * scale
        )
        dkey = (
            jnp.einsum("kgnm,nkgd->mkd", dscore, query4, preferred_element_type=jnp.float32) * scale
        )
        dvalue = jnp.einsum("kgnm,nkgd->mkd", prob_low, grad4, preferred_element_type=jnp.float32)
        both = jnp.concatenate(
            [dkey.reshape(keys_blk.shape[0], width), dvalue.reshape(keys_blk.shape[0], width)],
            axis=1,
        )
        return (dquery, both)

    def back_step(acc, blk):
        keys_blk, values_blk, key_pos = blk
        dquery, both = grads_block(keys_blk, values_blk, key_pos)
        return (acc + dquery, both)

    dquery0 = jnp.zeros((rows, HK, group, DH), jnp.float32)
    dquery, prompt_terms = scan_blocks(prompt_kbuf, prompt_vbuf, prompt_pos, back_step, dquery0)
    prompt_term = prompt_terms.reshape(prompt_rows, 2 * width)
    dquery, resp_terms = scan_blocks(resp_kbuf, resp_vbuf, resp_pos, back_step, dquery)
    resp_sum = lax.psum_scatter(
        resp_terms.reshape(seq_rows, 2 * width), "ctx", scatter_dimension=0, tiled=True
    )
    query_grad = dquery.reshape(rows, HQ * DH).astype(jnp.bfloat16)
    prompt_part = lax.psum_scatter(prompt_term, "ctx", scatter_dimension=0, tiled=True)
    prompt_sum = lax.psum(prompt_part, "resp")
    resp_key_grad = resp_sum[:, :width].astype(jnp.bfloat16)
    resp_value_grad = resp_sum[:, width:].astype(jnp.bfloat16)
    prompt_key_grad = prompt_sum[:, :width].astype(jnp.bfloat16)
    prompt_value_grad = prompt_sum[:, width:].astype(jnp.bfloat16)
    return (
        attn_out[None],
        query_grad[None],
        resp_key_grad[None],
        resp_value_grad[None],
        prompt_key_grad,
        prompt_value_grad,
    )


def solution(mesh):
    in_specs = (
        P("resp", "ctx", None),
        P("resp", "ctx", None),
        P("resp", "ctx", None),
        P("ctx", None),
        P("ctx", None),
        P("resp", "ctx", None),
        P("resp"),
    )
    out_specs = (
        P("resp", "ctx", None),
        P("resp", "ctx", None),
        P("resp", "ctx", None),
        P("resp", "ctx", None),
        P("ctx", None),
        P("ctx", None),
    )
    return jax.shard_map(body, mesh=mesh, in_specs=in_specs, out_specs=out_specs, check_vma=False)
```

profile of v0, /device:TPU:8, one launch (start us, length us, event | category | flops | bytes accessed | tf_op | source)
XLA Modules:
  0.0 321.6 jit_solution(5401829585454170042)
XLA Ops:
  7.2 1.7 copy.163
  11.4 23.7 %all_gather.12 = bf16[512,512]{1,0:T(8,128)(2,1)S(1)} all-gather(bf16[32,512]{1,0:T(8,128)(2,1)} %param.14), channel_id=1, replica_groups=mesh['resp'=16,'ctx'=16] {'ctx'}, dimensions={0}, use_global_device_ids=true | all-gather | bytes 557056 | tf_op jit(solution)/shard_map/all_gather | solution.py:59
  35.3 20.1 %all_gather.14 = bf16[512,512]{1,0:T(8,128)(2,1)S(1)} all-gather(bf16[32,512]{1,0:T(8,128)(2,1)} %param.15), channel_id=1, replica_groups=mesh['resp'=16,'ctx'=16] {'ctx'}, dimensions={0}, use_global_device_ids=true | all-gather | bytes 557056 | tf_op jit(solution)/shard_map/all_gather | solution.py:60
  58.5 3.2 bitcast_reduce_fusion
  61.7 4.8 %fusion.39 = (f32[4,5,128]{2,1,0:T(8,128)S(1)}, f32[4,2048,128,5]{2,1,3,0:T(8,128)S(1)}) fusion(pred[128,2048]{0,1:T(8,128)(4,1)S(1)} %iota_compare_fusion, bf16[2048,4,128,1]{0,2,3,1:T(8,128)(2,1)} %bitcast.261, bf16[128,4,5,128]{0,3,2,1:T(8,128)(2,1)S(1)} %bitcast.245), kind=kOutput, calls=%fused_computation.49 | convolution fusion | flops 1357903360 | bytes 23996416 | tf_op jit(solution)/shard_map/nkgd,mkd->kgnm/dot_general | solution.py:15
  66.5 3.7 %fusion.43 = f32[4,5,128]{2,1,0:T(8,128)S(1)} fusion(f32[4,512,128,5]{2,1,3,0:T(8,128)} %get-tuple-element.374, f32[4,5,128]{2,1,0:T(8,128)S(1)} %get-tuple-element.371, pred[128]{0:T(512)(128)(4,1)S(1)} %broadcast_compare_fusion.2), kind=kLoop, calls=%fused_computation.56 | loop fusion | flops 5240320 | bytes 5263488 | tf_op jit(solution)/shard_map/reduce_sum | solution.py:51
  70.2 4.5 %exponential_reduce_fusion = f32[4,5,128]{2,1,0:T(8,128)S(1)} fusion(f32[4,2048,128,5]{2,1,3,0:T(8,128)S(1)} %get-tuple-element.376, f32[4,5,128]{2,1,0:T(8,128)S(1)} %get-tuple-element.372, pred[128,2048]{0,1:T(8,128)(4,1)S(1)} %iota_compare_fusion), kind=kLoop, calls=%fused_computation.48 | loop fusion | flops 20968960 | bytes 21254144 | tf_op jit(solution)/shard_map/reduce_sum | solution.py:51
  75.4 2.6 convolution_bitcast_fusion.1
  77.9 1.7 copy.169
  79.6 4.5 %reshape.290 = bf16[4,512,512]{1,0,2:T(4,128)(2,1)} reshape(bf16[1,2048,512]{1,2,0:T(8,128)(2,1)} %all-gather.5.cloned.1.call-done) | data formatting | bytes 4194304 | tf_op jit(solution)/shard_map/reshape | solution.py:25
  84.1 3.3 %copy.171 = bf16[4,512,512]{1,2,0:T(8,128)(2,1)} copy(bf16[4,512,512]{1,0,2:T(4,128)(2,1)} %reshape.290) | data formatting | bytes 4194304
  87.5 6.5 %all-gather.7.cloned.1.call-done = bf16[1,2048,512]{2,1,0:T(8,128)(2,1)} async-done(((bf16[1,128,512]{2,1,0:T(8,128)(2,1)}), bf16[1,2048,512]{2,1,0:T(8,128)(2,1)}) %all-gather.7.cloned.1.call-update) | async-done | bytes 2097168 | tf_op jit(solution)/shard_map/all_gather | solution.py:71
  93.9 4.1 %copy.170 = bf16[4,512,512]{1,2,0:T(8,128)(2,1)} copy(bf16[4,512,512]{2,1,0:T(8,128)(2,1)} %bitcast.267) | data formatting | bytes 4194304
  98.1 21.0 %while.6 = (s32[]{:T(128)}, f32[128,4,5,128]{0,3,2,1:T(8,128)S(1)}, bf16[4,512,512]{1,2,0:T(8,128)(2,1)}, s32[4,512]{1,0:T(4,128)S(1)}, bf16[4,512,512]{1,2,0:T(...) while((s32[]{:T(128)}, ...), condition=%wide.region_5.6_spmd.clone, body=%wide.region_4.5_spmd.clone.sunk | while | flops 676724864 | bytes 6571113 | solution.py:29
  100.1 3.1 fusion.108
  105.3 3.1 fusion.108
  110.6 3.1 fusion.108
  115.8 3.1 fusion.108
  119.2 1.9 fusion.48
  121.1 5.3 %fusion.50 = f32[4,128,512,1]{2,1,3,0:T(8,128)} fusion(bf16[128,4,5,128]{0,3,2,1:T(8,128)(2,1)S(1)} %get-tuple-element.536, f32[4,512,128,5]{2,1,3,0:T(8,128)} %get-tuple-element.374, f32[4,5,128]{2,1,0:T(8,128)} %get-tuple-element.581, pred[128]{0:T(512)(128)(4,1)S(1)} %broadcast_compare_fusion.3), kind=kOutput, calls=%fused_computation.75 | convolution fusion | flops 340787200 | bytes 6957184 | tf_op jit(solution)/shard_map/while/body/eval_jaxpr/kgnm,nkgd->mkd/dot_general | solution.py:125
  126.4 1.6 fusion.41
  130.1 2.5 copy.186
  133.9 3.1 pad_maximum_fusion
  137.1 1.5 copy.179
  138.6 69.7 %while.7 = (s32[]{:T(128)}, f32[128,4,5,128]{0,3,2,1:T(8,128)}, f32[4,512,1024]{2,1,0:T(8,128)}, bf16[4,512,512]{1,2,0:T(8,128)(2,1)}, s32[4,512]{1,0:T(4,128)S(...) while((s32[]{:T(128)}, f32[128,4,5,128]{0,3,2,1:T(8,128)}, ...), condition=%wide.region_7.8_spmd.clone, body=%wide.region_6.7_spmd.clone.sunk | while | flops 1692336256 | bytes 52139704 | solution.py:29
  141.0 1.7 fusion.120
  143.7 1.4 fusion.122
  145.1 1.5 maximum_bitcast_fusion.2
  146.7 2.9 copy.245
  149.6 3.2 constant_dynamic-update-slice_fusion.2
  152.8 3.2 fusion.121
  158.4 1.7 fusion.120
  162.5 1.5 maximum_bitcast_fusion.2
  164.1 2.9 copy.245
  167.0 3.2 constant_dynamic-update-slice_fusion.2
  170.2 3.2 fusion.121
  175.8 1.7 fusion.120
  179.9 1.5 maximum_bitcast_fusion.2
  181.5 2.9 copy.245
  184.4 3.2 constant_dynamic-update-slice_fusion.2
  187.6 3.2 fusion.121
  193.2 1.7 fusion.120
  197.4 1.5 maximum_bitcast_fusion.2
  198.9 2.9 copy.245
  201.8 3.2 constant_dynamic-update-slice_fusion.2
  205.0 3.2 fusion.121
  211.9 81.9 %all-reduce.1 = bf16[32,1024]{1,0:T(8,128)(2,1)S(1)} all-reduce(f32[32,1024]{1,0:T(8,128)} %reduce-scatter.5.cloned.1.call-done), channel_id=1, replica_groups=mesh['resp'=16,'ctx'=16] {'resp'}, use_global_device_ids=true, to_apply=%region_10.11 | all-reduce | flops 32768 | bytes 196608 | tf_op jit(solution)/shard_map/psum | solution.py:146
  294.5 18.8 %reduce-scatter.3.cloned.1.call-done = f32[128,1024]{1,0:T(8,128)} async-done(((f32[2048,1024]{1,0:T(8,128)}), f32[128,1024]{1,0:T(8,128)}) %reduce-scatter.3.cloned.1.call-update) | async-done | bytes 524304 | tf_op jit(solution)/shard_map/reduce_scatter | solution.py:141
  (127 shorter events, 41.1 us)
Async XLA Ops:
  7.2 50.2 %copy-start.4 = (bf16[1,128,2560]{2,1,0:T(8,128)(2,1)S(1)}, bf16[1,128,2560]{2,1,0:T(8,128)(2,1)}, u32[]{:S(2)}) copy-start(bf16[1,128,2560]{2,1,0:T(8,128)(2,1)} %param.16) | copy-start | bytes 1966084
  7.2 54.5 %all-gather.5.cloned.1.call-start = ((), (), s32[]{:S(2)}) async-start(), calls=%async_computation.4 | async-start | bytes 2228224 | tf_op jit(solution)/shard_map/all_gather | solution.py:70
  9.0 85.0 %all-gather.7.cloned.1.call-start = ((), (), s32[]{:S(2)}) async-start(), calls=%async_computation.5 | async-start | bytes 2228224 | tf_op jit(solution)/shard_map/all_gather | solution.py:71
  9.7 202.2 %reduce-scatter.5.cloned.1.call-start = ((), (), s32[]{:S(2)}) async-start(), calls=%async_computation.3 | async-start | bytes 2228224 | tf_op jit(solution)/shard_map/reduce_scatter | solution.py:145
  55.6 19.1 %copy-start.7 = (bf16[512,512]{0,1:T(8,128)(2,1)}, bf16[512,512]{0,1:T(8,128)(2,1)S(1)}, u32[]{:S(2)}) copy-start(bf16[512,512]{0,1:T(8,128)(2,1)S(1)} %copy.166) | copy-start | bytes 1572868
  66.5 8.9 %slice-start = ((s8[5242880]{0:T(1024)(128)(4,1)}), s8[4194304]{0:T(1024)(128)(4,1)S(1)}, s32[]{:S(2)}) async-start(s8[5242880]{0:T(1024)(128)(4,1)} %bitcast.252), calls=%async_computation.6 | async-start | bytes 8388608
  70.2 5.2 %slice-start.1 = ((s8[5242880]{0:T(1024)(128)(4,1)}), s8[1048576]{0:T(1024)(128)(4,1)S(1)}, s32[]{:S(2)}) async-start(s8[5242880]{0:T(1024)(128)(4,1)} %bitcast.252), calls=%async_computation.7 | async-start | bytes 2097152
  74.8 0.6 copy-start.11
  119.1 7.2 %copy-start.2 = (f32[128,4,5,128]{0,3,2,1:T(8,128)}, f32[128,4,5,128]{0,3,2,1:T(8,128)S(1)}, u32[]{:S(2)}) copy-start(f32[128,4,5,128]{0,3,2,1:T(8,128)S(1)} %get-tuple-element.157) | copy-start | bytes 3932164
  119.1 7.2 %slice-start.2 = ((s8[5242880]{0:T(1024)(128)(4,1)}), s8[4194304]{0:T(1024)(128)(4,1)S(1)}, s32[]{:S(2)}) async-start(s8[5242880]{0:T(1024)(128)(4,1)} %bitcast.254), calls=%async_computation.8 | async-start | bytes 8388608
  119.1 7.2 %copy-start.8 = (bf16[512,512]{0,1:T(8,128)(2,1)S(1)}, bf16[512,512]{0,1:T(8,128)(2,1)}, u32[]{:S(2)}) copy-start(bf16[512,512]{0,1:T(8,128)(2,1)} %copy-done.7) | copy-start | bytes 1572868
  119.1 7.2 %copy-start.12 = (f32[4,5,128]{2,1,0:T(8,128)S(1)}, f32[4,5,128]{2,1,0:T(8,128)}, u32[]{:S(2)}) copy-start(f32[4,5,128]{2,1,0:T(8,128)} %get-tuple-element.581) | copy-start | bytes 30724
  121.0 7.0 %copy-start.5 = (bf16[128,4,5,128]{0,3,2,1:T(8,128)(2,1)}, bf16[128,4,5,128]{0,3,2,1:T(8,128)(2,1)S(1)}, u32[]{:S(2)}) copy-start(bf16[128,4,5,128]{0,3,2,1:T(8,128)(2,1)S(1)} %get-tuple-element.536) | copy-start | bytes 1966084
  121.0 7.0 %copy-start.9 = (f32[4,5,128]{2,1,0:T(8,128)}, f32[4,5,128]{2,1,0:T(8,128)S(1)}, u32[]{:S(2)}) copy-start(f32[4,5,128]{2,1,0:T(8,128)S(1)} %get-tuple-element.537) | copy-start | bytes 30724
  121.1 5.3 %slice-start.3 = ((s8[5242880]{0:T(1024)(128)(4,1)}), s8[1048576]{0:T(1024)(128)(4,1)S(1)}, s32[]{:S(2)}) async-start(s8[5242880]{0:T(1024)(128)(4,1)} %bitcast.254), calls=%async_computation.9 | async-start | bytes 2097152
  132.6 5.9 %copy-start.10 = (f32[4,5,128]{2,1,0:T(8,128)S(1)}, f32[4,5,128]{2,1,0:T(8,128)}, u32[]{:S(2)}) copy-start(f32[4,5,128]{2,1,0:T(8,128)} %copy-done.9) | copy-start | bytes 30724
  132.6 5.9 %copy-start.13 = (f32[4,5,128]{2,1,0:T(8,128)S(1)}, f32[4,5,128]{2,1,0:T(8,128)}, u32[]{:S(2)}) copy-start(f32[4,5,128]{2,1,0:T(8,128)} %get-tuple-element.581) | copy-start | bytes 30724
  137.0 176.3 %reduce-scatter.3.cloned.1.call-start = ((), (), s32[]{:S(2)}) async-start(), calls=%async_computation.2 | async-start | bytes 8912896 | tf_op jit(solution)/shard_map/reduce_scatter | solution.py:141
  138.6 2.4 copy-start.6
  139.9 1.1 copy-start
  156.0 2.4 copy-start.6
  157.3 1.1 copy-start
  173.4 2.4 copy-start.6
  174.7 1.1 copy-start
  190.8 2.4 copy-start.6
  192.1 1.1 copy-start
  208.2 1.3 copy-start.1
  208.2 2.5 copy-start.3
Sparse Core Ops, SparseCore 0:
  10.4 43.8 all-gather.4
  56.1 37.7 all-gather.6
  137.1 66.8 reduce-scatter.4
  208.4 104.8 reduce-scatter.2
where the time goes:
time: 323 us; the launch traced here: 322 us
  blocking collectives  126 us (39%)
  local copies, waits for them, and re-layouts  65.2 us (20%)
  matrix products  64.7 us (20%)
  waiting for transfers between devices  26 us (8%)
  other arithmetic  24.4 us (8%)
  between operations  14.7 us (5%)
    psum x1, blocking collectives, body(): prompt_sum = lax.psum(prompt_part, 'resp')  81.9 us
    dynamic_update_slice x8, local copies, waits for them, and re-layouts, scan_blocks(): return lax.scan(step, init, blocks)  24.5 us
    all_gather x1, blocking collectives, body(): lax.all_gather(prompt_keys, 'ctx', axis=0, tiled=True)  23.7 us
    all_gather x1, blocking collectives, body(): lax.all_gather(prompt_values, 'ctx', axis=0, tiled=True)  20.1 us
    unnamed x42, local copies, waits for them, and re-layouts  20 us
    reduce_scatter x1, waiting for transfers between devices, body(): lax.psum_scatter(resp_terms.reshape(seq_rows, 2 * width), 'ctx', scatter_...  18.8 us
    dot_general x5, matrix products, out_step(): jnp.einsum('kgnm,mkd->nkgd', prob, values3, preferred_element_type=jnp.fl...  15.1 us
    dot_general x5, matrix products, grads_block(): jnp.einsum('kgnm,mkd->nkgd', dscore, keys3, preferred_element_type=jnp.fl...  13.8 us
  transfers between devices with their start and end apart: 4, of which 2 were waited for; matrix products, arithmetic and copies ran while one was open for 33% of the time, Pallas kernels for 0%

commit v1 on v0

--- a/solution.py
+++ b/solution.py
@@ -8,6 +8,9 @@
 HQ = 20
 HK = 4
 NEG = -1e30
+move_the_ladders = lambda vector, mesh_ax, dimension_no: jnp.concatenate(
+    lax.all_to_all(jnp.stack([vector] * lax.axis_size(mesh_ax), 0), mesh_ax, 0, 0), dimension_no
+)
 
 
 def score_block(query4, keys_blk, key_pos, row_pos, scale):
@@ -68,7 +71,7 @@
     top, total, prompt_kbuf, prompt_vbuf = (top, total, key_buf, value_buf)
     pieces = (
         lax.all_gather(resp_keys[0], "ctx", axis=0, tiled=True),
-        lax.all_gather(resp_values[0], "ctx", axis=0, tiled=True),
+        move_the_ladders(resp_values[0], "ctx", 0),
     )
     top, total, key_buf, value_buf = (
         top,

time: 323 us -> 347 us (1.074)
  blocking collectives: 126 us -> 152 us
  waiting for transfers between devices: 26 us -> 16.8 us
  starting transfers between devices: 0.16 us -> 6.06 us
    all_gather x1, blocking collectives: 23.7 us -> 46.6 us  [body(): lax.all_gather(prompt_keys, 'ctx', axis=0, tiled=True)]
    all_gather x1 -> x0, waiting for transfers between devices: 6.47 us -> none  [body(): lax.all_gather(resp_values[0], 'ctx', axis=0, tiled=True)]
    all_to_all x0 -> x1, starting transfers between devices: none -> 5.94 us  [lax.all_to_all(jnp.stack([vector] * lax.axis_size(mesh_ax), 0), mesh_ax,...]
    unnamed x42 -> x48, local copies, waits for them, and re-layouts: 20 us -> 19 us
  transfers between devices with their start and end apart: 4 -> 4, of which waited for: 2 -> 1; matrix products, arithmetic and copies ran while one was open for 33% -> 31% of each run, Pallas kernels for 0% -> 0%
where the time goes in v1:
time: 347 us; the launch traced here: 346 us
  blocking collectives  152 us (44%)
  local copies, waits for them, and re-layouts  66.5 us (19%)
  matrix products  65 us (19%)
  other arithmetic  24.3 us (7%)
  waiting for transfers between devices  16.8 us (5%)
  between operations  14.8 us (4%)
  starting transfers between devices  6.06 us (2%)
    psum x1, blocking collectives, body(): prompt_sum = lax.psum(prompt_part, 'resp')  84.3 us
    all_gather x1, blocking collectives, body(): lax.all_gather(prompt_keys, 'ctx', axis=0, tiled=True)  46.6 us
    dynamic_update_slice x8, local copies, waits for them, and re-layouts, scan_blocks(): return lax.scan(step, init, blocks)  24.4 us
    all_gather x1, blocking collectives, body(): lax.all_gather(prompt_values, 'ctx', axis=0, tiled=True)  21.3 us
    unnamed x48, local copies, waits for them, and re-layouts  19 us
    reduce_scatter x1, waiting for transfers between devices, body(): lax.psum_scatter(resp_terms.reshape(seq_rows, 2 * width), 'ctx', scatter_...  16.7 us
    dot_general x5, matrix products, out_step(): jnp.einsum('kgnm,mkd->nkgd', prob, values3, preferred_element_type=jnp.fl...  15.1 us
    dot_general x5, matrix products, grads_block(): jnp.einsum('kgnm,mkd->nkgd', dscore, keys3, preferred_element_type=jnp.fl...  14 us
  transfers between devices with their start and end apart: 4, of which 1 were waited for; matrix products, arithmetic and copies ran while one was open for 31% of the time, Pallas kernels for 0%

profile of v1, /device:TPU:8, one launch (start us, length us, event | category | flops | bytes accessed | tf_op | source)
XLA Modules:
  0.0 346.2 jit_solution(865267304290936259)
XLA Ops:
  7.2 1.7 copy.163
  9.0 2.4 stack.3
  11.4 5.9 %all-to-all-start = ((bf16[16,128,512]{2,1,0:T(8,128)(2,1)}), bf16[16,128,512]{2,1,0:T(8,128)(2,1)}, u32[]{:S(2)}, u32[]{:S(2)}) async-start(bf16[16,128,512]{2,1,0:T(8,128)(2,1)} %stack.3), calls=%async_computation | async-start | bytes 4194304 | tf_op jit(solution)/shard_map/all_to_all | solution.py:12
  17.8 46.6 %all_gather.9 = bf16[512,512]{1,0:T(8,128)(2,1)S(1)} all-gather(bf16[32,512]{1,0:T(8,128)(2,1)S(1)} %copy-done.10), channel_id=1, replica_groups=mesh['resp'=16,'ctx'=16] {'ctx'}, dimensions={0}, use_global_device_ids=true | all-gather | bytes 557056 | tf_op jit(solution)/shard_map/all_gather | solution.py:62
  64.6 21.3 %all_gather.11 = bf16[512,512]{1,0:T(8,128)(2,1)S(1)} all-gather(bf16[32,512]{1,0:T(8,128)(2,1)S(1)} %copy-done.11), channel_id=1, replica_groups=mesh['resp'=16,'ctx'=16] {'ctx'}, dimensions={0}, use_global_device_ids=true | all-gather | bytes 557056 | tf_op jit(solution)/shard_map/all_gather | solution.py:63
  89.2 3.3 bitcast_reduce_fusion
  92.5 4.8 %fusion.39 = (f32[4,5,128]{2,1,0:T(8,128)S(1)}, f32[4,2048,128,5]{2,1,3,0:T(8,128)S(1)}) fusion(pred[128,2048]{0,1:T(8,128)(4,1)S(1)} %iota_compare_fusion, bf16[2048,4,128,1]{0,2,3,1:T(8,128)(2,1)} %bitcast.262, bf16[128,4,5,128]{0,3,2,1:T(8,128)(2,1)S(1)} %bitcast.246), kind=kOutput, calls=%fused_computation.49 | convolution fusion | flops 1357903360 | bytes 23996416 | tf_op jit(solution)/shard_map/nkgd,mkd->kgnm/dot_general | solution.py:18
  97.4 3.7 %fusion.43 = f32[4,5,128]{2,1,0:T(8,128)S(1)} fusion(f32[4,512,128,5]{2,1,3,0:T(8,128)} %get-tuple-element.374, f32[4,5,128]{2,1,0:T(8,128)S(1)} %get-tuple-element.371, pred[128]{0:T(512)(128)(4,1)S(1)} %broadcast_compare_fusion.2), kind=kLoop, calls=%fused_computation.56 | loop fusion | flops 5240320 | bytes 5263488 | tf_op jit(solution)/shard_map/reduce_sum | solution.py:54
  101.0 4.5 %exponential_reduce_fusion = f32[4,5,128]{2,1,0:T(8,128)S(1)} fusion(f32[4,2048,128,5]{2,1,3,0:T(8,128)S(1)} %get-tuple-element.376, f32[4,5,128]{2,1,0:T(8,128)S(1)} %get-tuple-element.372, pred[128,2048]{0,1:T(8,128)(4,1)S(1)} %iota_compare_fusion), kind=kLoop, calls=%fused_computation.48 | loop fusion | flops 20968960 | bytes 21254144 | tf_op jit(solution)/shard_map/reduce_sum | solution.py:54
  106.2 2.6 convolution_bitcast_fusion.1
  108.8 1.7 copy.169
  110.5 4.5 %reshape.286 = bf16[4,512,512]{1,0,2:T(4,128)(2,1)} reshape(bf16[1,2048,512]{1,2,0:T(8,128)(2,1)} %all-gather.3.cloned.1.call-done) | data formatting | bytes 4194304 | tf_op jit(solution)/shard_map/reshape | solution.py:28
  115.0 3.3 copy.171
  118.3 4.1 %copy.170 = bf16[4,512,512]{1,2,0:T(8,128)(2,1)} copy(bf16[4,512,512]{2,1,0:T(8,128)(2,1)} %bitcast.15) | data formatting | bytes 4194304
  122.4 21.0 %while.6 = (s32[]{:T(128)}, f32[128,4,5,128]{0,3,2,1:T(8,128)S(1)}, bf16[4,512,512]{1,2,0:T(8,128)(2,1)}, s32[4,512]{1,0:T(4,128)S(1)}, bf16[4,512,512]{1,2,0:T(...) while((s32[]{:T(128)}, ...), condition=%wide.region_5.6_spmd.clone, body=%wide.region_4.5_spmd.clone.sunk | while | flops 676724864 | bytes 6571113 | solution.py:32
  124.5 3.1 fusion.108
  129.7 3.1 fusion.108
  134.9 3.1 fusion.108
  140.2 3.1 fusion.108
  143.5 1.9 fusion.48
  145.4 5.2 %fusion.50 = f32[4,128,512,1]{2,1,3,0:T(8,128)} fusion(bf16[128,4,5,128]{0,3,2,1:T(8,128)(2,1)S(1)} %get-tuple-element.536, f32[4,512,128,5]{2,1,3,0:T(8,128)} %get-tuple-element.374, f32[4,5,128]{2,1,0:T(8,128)} %get-tuple-element.577, pred[128]{0:T(512)(128)(4,1)S(1)} %broadcast_compare_fusion.3), kind=kOutput, calls=%fused_computation.75 | convolution fusion | flops 340787200 | bytes 6957184 | tf_op jit(solution)/shard_map/while/body/eval_jaxpr/kgnm,nkgd->mkd/dot_general | solution.py:128
  150.7 1.6 fusion.41
  154.4 2.6 copy.186
  158.2 3.2 pad_maximum_fusion
  161.5 1.5 copy.179
  163.0 69.5 %while.7 = (s32[]{:T(128)}, f32[128,4,5,128]{0,3,2,1:T(8,128)}, f32[4,512,1024]{2,1,0:T(8,128)}, bf16[4,512,512]{1,2,0:T(8,128)(2,1)}, s32[4,512]{1,0:T(4,128)S(...) while((s32[]{:T(128)}, f32[128,4,5,128]{0,3,2,1:T(8,128)}, ...), condition=%wide.region_7.8_spmd.clone, body=%wide.region_6.7_spmd.clone.sunk | while | flops 1692336256 | bytes 52139704 | solution.py:32
  165.4 1.7 fusion.120
  169.6 1.5 maximum_bitcast_fusion.2
  171.0 2.9 copy.245
  173.9 3.2 constant_dynamic-update-slice_fusion.2
  177.1 3.2 fusion.121
  182.8 1.7 fusion.120
  186.9 1.5 maximum_bitcast_fusion.2
  188.4 2.9 copy.245
  191.3 3.2 constant_dynamic-update-slice_fusion.2
  194.5 3.2 fusion.121
  200.1 1.7 fusion.120
  204.3 1.5 maximum_bitcast_fusion.2
  205.7 2.9 copy.245
  208.7 3.2 constant_dynamic-update-slice_fusion.2
  211.9 3.2 fusion.121
  217.5 1.7 fusion.120
  221.7 1.5 maximum_bitcast_fusion.2
  223.1 2.9 copy.245
  226.1 3.2 constant_dynamic-update-slice_fusion.2
  229.3 3.2 fusion.121
  236.2 84.3 %all-reduce.1 = bf16[32,1024]{1,0:T(8,128)(2,1)S(1)} all-reduce(f32[32,1024]{1,0:T(8,128)} %reduce-scatter.5.cloned.1.call-done), channel_id=1, replica_groups=mesh['resp'=16,'ctx'=16] {'resp'}, use_global_device_ids=true, to_apply=%region_10.11 | all-reduce | flops 32768 | bytes 196608 | tf_op jit(solution)/shard_map/psum | solution.py:149
  321.1 16.7 %reduce-scatter.3.cloned.1.call-done = f32[128,1024]{1,0:T(8,128)} async-done(((f32[2048,1024]{1,0:T(8,128)}), f32[128,1024]{1,0:T(8,128)}) %reduce-scatter.3.cloned.1.call-update) | async-done | bytes 524304 | tf_op jit(solution)/shard_map/reduce_scatter | solution.py:144
  (133 shorter events, 40.7 us)
Async XLA Ops:
  7.2 10.3 %copy-start.4 = (bf16[1,128,2560]{2,1,0:T(8,128)(2,1)S(1)}, bf16[1,128,2560]{2,1,0:T(8,128)(2,1)}, u32[]{:S(2)}) copy-start(bf16[1,128,2560]{2,1,0:T(8,128)(2,1)} %param.11) | copy-start | bytes 1966084
  7.2 10.6 %copy-start.10 = (bf16[32,512]{1,0:T(8,128)(2,1)S(1)}, bf16[32,512]{1,0:T(8,128)(2,1)}, u32[]{:S(2)}) copy-start(bf16[32,512]{1,0:T(8,128)(2,1)} %param.14) | copy-start | bytes 98308
  7.2 57.4 %copy-start.11 = (bf16[32,512]{1,0:T(8,128)(2,1)S(1)}, bf16[32,512]{1,0:T(8,128)(2,1)}, u32[]{:S(2)}) copy-start(bf16[32,512]{1,0:T(8,128)(2,1)} %param.15) | copy-start | bytes 98308
  7.2 85.3 %all-gather.3.cloned.1.call-start = ((), (), s32[]{:S(2)}) async-start(), calls=%async_computation.5 | async-start | bytes 2228224 | tf_op jit(solution)/shard_map/all_gather | solution.py:73
  11.4 76.5 %copy-start.5 = (bf16[1,128,2560]{2,1,0:T(8,128)(2,1)S(1)}, bf16[1,128,2560]{2,1,0:T(8,128)(2,1)}, u32[]{:S(2)}) copy-start(bf16[1,128,2560]{2,1,0:T(8,128)(2,1)} %param.16) | copy-start | bytes 1966084
  11.4 106.9 %all-to-all-start = ((bf16[16,128,512]{2,1,0:T(8,128)(2,1)}), bf16[16,128,512]{2,1,0:T(8,128)(2,1)}, u32[]{:S(2)}, u32[]{:S(2)}) async-start(bf16[16,128,512]{2,1,0:T(8,128)(2,1)} %stack.3), calls=%async_computation | async-start | bytes 4194304 | tf_op jit(solution)/shard_map/all_to_all | solution.py:12
  17.4 218.9 %reduce-scatter.5.cloned.1.call-start = ((), (), s32[]{:S(2)}) async-start(), calls=%async_computation.4 | async-start | bytes 2228224 | tf_op jit(solution)/shard_map/reduce_scatter | solution.py:148
  86.1 19.5 %copy-start.8 = (bf16[512,512]{0,1:T(8,128)(2,1)}, bf16[512,512]{0,1:T(8,128)(2,1)S(1)}, u32[]{:S(2)}) copy-start(bf16[512,512]{0,1:T(8,128)(2,1)S(1)} %copy.166) | copy-start | bytes 1572868
  97.3 8.9 %slice-start = ((s8[5242880]{0:T(1024)(128)(4,1)}), s8[4194304]{0:T(1024)(128)(4,1)S(1)}, s32[]{:S(2)}) async-start(s8[5242880]{0:T(1024)(128)(4,1)} %bitcast.253), calls=%async_computation.6 | async-start | bytes 8388608
  101.0 5.2 %slice-start.1 = ((s8[5242880]{0:T(1024)(128)(4,1)}), s8[1048576]{0:T(1024)(128)(4,1)S(1)}, s32[]{:S(2)}) async-start(s8[5242880]{0:T(1024)(128)(4,1)} %bitcast.253), calls=%async_computation.7 | async-start | bytes 2097152
  105.6 0.6 copy-start.14
  143.5 7.2 %copy-start.2 = (f32[128,4,5,128]{0,3,2,1:T(8,128)}, f32[128,4,5,128]{0,3,2,1:T(8,128)S(1)}, u32[]{:S(2)}) copy-start(f32[128,4,5,128]{0,3,2,1:T(8,128)S(1)} %get-tuple-element.157) | copy-start | bytes 3932164
  143.5 7.2 %slice-start.2 = ((s8[5242880]{0:T(1024)(128)(4,1)}), s8[4194304]{0:T(1024)(128)(4,1)S(1)}, s32[]{:S(2)}) async-start(s8[5242880]{0:T(1024)(128)(4,1)} %bitcast.255), calls=%async_computation.8 | async-start | bytes 8388608
  143.5 7.1 %copy-start.9 = (bf16[512,512]{0,1:T(8,128)(2,1)S(1)}, bf16[512,512]{0,1:T(8,128)(2,1)}, u32[]{:S(2)}) copy-start(bf16[512,512]{0,1:T(8,128)(2,1)} %copy-done.8) | copy-start | bytes 1572868
  143.5 7.1 %copy-start.15 = (f32[4,5,128]{2,1,0:T(8,128)S(1)}, f32[4,5,128]{2,1,0:T(8,128)}, u32[]{:S(2)}) copy-start(f32[4,5,128]{2,1,0:T(8,128)} %get-tuple-element.577) | copy-start | bytes 30724
  145.4 6.9 %copy-start.6 = (bf16[128,4,5,128]{0,3,2,1:T(8,128)(2,1)}, bf16[128,4,5,128]{0,3,2,1:T(8,128)(2,1)S(1)}, u32[]{:S(2)}) copy-start(bf16[128,4,5,128]{0,3,2,1:T(8,128)(2,1)S(1)} %get-tuple-element.536) | copy-start | bytes 1966084
  145.4 6.9 %copy-start.12 = (f32[4,5,128]{2,1,0:T(8,128)}, f32[4,5,128]{2,1,0:T(8,128)S(1)}, u32[]{:S(2)}) copy-start(f32[4,5,128]{2,1,0:T(8,128)S(1)} %get-tuple-element.537) | copy-start | bytes 30724
  145.4 5.2 %slice-start.3 = ((s8[5242880]{0:T(1024)(128)(4,1)}), s8[1048576]{0:T(1024)(128)(4,1)S(1)}, s32[]{:S(2)}) async-start(s8[5242880]{0:T(1024)(128)(4,1)} %bitcast.255), calls=%async_computation.9 | async-start | bytes 2097152
  156.9 6.0 %copy-start.13 = (f32[4,5,128]{2,1,0:T(8,128)S(1)}, f32[4,5,128]{2,1,0:T(8,128)}, u32[]{:S(2)}) copy-start(f32[4,5,128]{2,1,0:T(8,128)} %copy-done.12) | copy-start | bytes 30724
  156.9 6.0 %copy-start.16 = (f32[4,5,128]{2,1,0:T(8,128)S(1)}, f32[4,5,128]{2,1,0:T(8,128)}, u32[]{:S(2)}) copy-start(f32[4,5,128]{2,1,0:T(8,128)} %get-tuple-element.577) | copy-start | bytes 30724
  161.4 176.4 %reduce-scatter.3.cloned.1.call-start = ((), (), s32[]{:S(2)}) async-start(), calls=%async_computation.3 | async-start | bytes 8912896 | tf_op jit(solution)/shard_map/reduce_scatter | solution.py:144
  163.0 2.4 copy-start.7
  164.3 1.1 copy-start
  180.3 2.4 copy-start.7
  181.7 1.1 copy-start
  197.7 2.4 copy-start.7
  199.0 1.1 copy-start
  215.1 2.4 copy-start.7
  216.4 1.1 copy-start
  232.5 1.3 copy-start.1
  232.5 2.5 copy-start.3
Sparse Core Ops, SparseCore 0:
  10.4 55.6 all-gather.2
  161.5 67.2 reduce-scatter.4
  232.7 105.1 reduce-scatter.2
